TPU v7x, 128 devices: a whole 4x4x4 slice. The times are simulated.
128 devices in a mesh: row: 8 (over y, x_hi), col: 16 (over z, x_lo, core).
Axes of the slice: x: 4 (x_hi: 2, x_lo: 2; x = x_hi * 2 + x_lo), y: 4, z: 4, core: 2. Of those that a mesh axis runs over, the one named last changes fastest.
Arguments:
- new_row: float32 [128, 192, 128], P('row', 'col'), may hold values from -4 to 4
- history: float32 [192, 192, 128, 128], P('row', 'col'), may hold values from -0.0390625 to 0.0390625
- hamiltonian: float32 [128, 128], replicated, may hold values from -0.5 to 0.5
Outputs:
- rows_out: float32 [3, 128, 192, 128], P(None, 'row', 'col')
All inputs are finite; a program needn't handle non-finite values.
Results may differ from a plain program's by a relative error of at most 0.00026.
Values sent between devices are 32-bit elements; how exact they have to be, the bound alone decides.
A program may use at most 128 MiB of HBM per device.

v0:
```python
import jax
import jax.numpy as jnp
from jax import lax
from jax.sharding import PartitionSpec as P

STEPS = 3


time_step = 0.2


def sigma_panel(sigma_all, tile_rows):
    row_start = lax.axis_index("row") * tile_rows
    gathered = lax.all_gather(sigma_all, "col", axis=1, tiled=True)
    return lax.dynamic_slice_in_dim(gathered, row_start, tile_rows, 1)


def contract(sigma_rows, history):
    return jnp.einsum(
        "isl,stlj->itj",
        sigma_rows,
        history,
        precision=lax.Precision.HIGHEST,
        preferred_element_type=jnp.float32,
    )


def advance(current, hamiltonian, collision):
    kinetic = jnp.einsum(
        "itl,lj->itj",
        current,
        hamiltonian,
        precision=lax.Precision.HIGHEST,
        preferred_element_type=jnp.float32,
    )
    return current - time_step * (kinetic + collision)


def per_device(new_row, history, hamiltonian):
    tile_rows = history.shape[0]
    results = []
    current = new_row
    for step_index in range(STEPS):
        sigma_local = current * current * current
        sigma_all = lax.all_gather(sigma_local, "row", axis=0, tiled=True)
        sigma_rows = sigma_panel(sigma_all, tile_rows)
        collision = lax.psum_scatter(
            contract(sigma_rows, history), "row", scatter_dimension=0, tiled=True
        )
        current = advance(current, hamiltonian, collision)
        results.append(current)
    return jnp.stack(results)


def solution(mesh):
    placed = (P("row", "col", None), P("row", "col", None, None), P())
    return jax.shard_map(
        per_device,
        mesh=mesh,
        in_specs=placed,
        out_specs=P(None, "row", "col", None),
        check_vma=False,
    )
```

profile of v0, /device:TPU:0, one launch (start us, length us, event | category | flops | bytes accessed | tf_op | source)
XLA Modules:
  0.0 612.5 jit_solution(13961219519606241692)
XLA Ops:
  6.5 0.0 copy-start
  6.5 0.0 copy-start.1
  6.5 0.0 all-gather.4.cloned.1.call-start
  6.5 1.0 multiply_multiply_fusion.2
  7.5 38.7 %all_gather.18 = f32[128,12,128]{2,0,1:T(8,128)} all-gather(f32[16,12,128]{2,0,1:T(8,128)S(1)} %multiply_multiply_fusion.2), channel_id=1, replica_groups=mesh['row'=8,'col'=16] {'row'}, dimensions={0}, use_global_device_ids=true | all-gather | bytes 884736 | tf_op jit(solution)/shard_map/all_gather | solution.py:45
  46.2 0.0 all-gather.4.cloned.1.call-update
  46.2 0.0 reduce-scatter.4.cloned.1.call-start
  46.3 74.7 %all-gather.4.cloned.1.call-done = f32[128,192,128]{2,0,1:T(8,128)} async-done(((f32[128,12,128]{2,0,1:T(8,128)}), f32[128,192,128]{2,0,1:T(8,128)}) %all-gather.4.cloned.1.call-update) | async-done | bytes 12582928 | tf_op jit(solution)/shard_map/all_gather | solution.py:14
  121.0 14.3 %fusion.9 = f32[128,12,128]{2,0,1:T(8,128)} fusion(f32[24,12,128,128]{3,2,1,0:T(8,128)} %param.4, f32[128,192,128]{2,0,1:T(8,128)} %all-gather.4.cloned.1.call-done, s32[]{:T(128)S(6)} %select_n.2), kind=kOutput, calls=%fused_computation.9 | convolution fusion | flops 7247757312 | bytes 21233668 | tf_op jit(solution)/shard_map/isl,stlj->itj/dot_general | solution.py:19
  135.3 0.0 reduce-scatter.4.cloned.1.call-update
  135.3 0.0 all-gather.6.cloned.1.call-start
  135.4 72.5 %reduce-scatter.4.cloned.1.call-done = f32[16,12,128]{2,0,1:T(8,128)} async-done(((f32[128,12,128]{2,0,1:T(8,128)}), f32[16,12,128]{2,0,1:T(8,128)}) %reduce-scatter.4.cloned.1.call-update) | async-done | bytes 98320 | tf_op jit(solution)/shard_map/reduce_scatter | solution.py:47
  207.8 0.0 copy-done
  207.9 0.0 copy-done.1
  207.9 1.1 multiply_multiply_fusion.1
  209.0 38.9 %all_gather.20 = f32[128,12,128]{2,0,1:T(8,128)} all-gather(f32[16,12,128]{2,0,1:T(8,128)S(1)} %get-tuple-element.5), channel_id=1, replica_groups=mesh['row'=8,'col'=16] {'row'}, dimensions={0}, use_global_device_ids=true | all-gather | bytes 884736 | tf_op jit(solution)/shard_map/all_gather | solution.py:45
  247.9 0.0 all-gather.6.cloned.1.call-update
  247.9 0.0 reduce-scatter.6.cloned.1.call-start
  248.0 71.0 %all-gather.6.cloned.1.call-done = f32[128,192,128]{2,0,1:T(8,128)} async-done(((f32[128,12,128]{2,0,1:T(8,128)}), f32[128,192,128]{2,0,1:T(8,128)}) %all-gather.6.cloned.1.call-update) | async-done | bytes 12582928 | tf_op jit(solution)/shard_map/all_gather | solution.py:14
  319.0 14.3 %fusion.12 = f32[128,12,128]{2,0,1:T(8,128)} fusion(f32[24,12,128,128]{3,2,1,0:T(8,128)} %param.4, f32[128,192,128]{2,0,1:T(8,128)} %all-gather.6.cloned.1.call-done, s32[]{:T(128)S(6)} %select_n.2), kind=kOutput, calls=%fused_computation.10 | convolution fusion | flops 7247757312 | bytes 21233668 | tf_op jit(solution)/shard_map/isl,stlj->itj/dot_general | solution.py:19
  333.3 0.0 reduce-scatter.6.cloned.1.call-update
  333.3 0.0 all-gather.8.cloned.1.call-start
  333.4 72.5 %reduce-scatter.6.cloned.1.call-done = f32[16,12,128]{2,0,1:T(8,128)} async-done(((f32[128,12,128]{2,0,1:T(8,128)}), f32[16,12,128]{2,0,1:T(8,128)}) %reduce-scatter.6.cloned.1.call-update) | async-done | bytes 98320 | tf_op jit(solution)/shard_map/reduce_scatter | solution.py:47
  405.9 1.1 multiply_multiply_fusion
  407.0 38.9 %all_gather.22 = f32[128,12,128]{2,0,1:T(8,128)} all-gather(f32[16,12,128]{2,0,1:T(8,128)S(1)} %get-tuple-element.7), channel_id=1, replica_groups=mesh['row'=8,'col'=16] {'row'}, dimensions={0}, use_global_device_ids=true | all-gather | bytes 884736 | tf_op jit(solution)/shard_map/all_gather | solution.py:45
  445.9 0.0 all-gather.8.cloned.1.call-update
  445.9 0.2 reduce-scatter.8.cloned.1.call-start
  446.2 70.8 %all-gather.8.cloned.1.call-done = f32[128,192,128]{2,0,1:T(8,128)} async-done(((f32[128,12,128]{2,0,1:T(8,128)}), f32[128,192,128]{2,0,1:T(8,128)}) %all-gather.8.cloned.1.call-update) | async-done | bytes 12582928 | tf_op jit(solution)/shard_map/all_gather | solution.py:14
  516.9 14.3 %fusion.15 = f32[128,12,128]{2,0,1:T(8,128)} fusion(f32[24,12,128,128]{3,2,1,0:T(8,128)} %param.4, f32[128,192,128]{2,0,1:T(8,128)} %all-gather.8.cloned.1.call-done, s32[]{:T(128)S(6)} %select_n.2), kind=kOutput, calls=%fused_computation.11 | convolution fusion | flops 7247757312 | bytes 21233668 | tf_op jit(solution)/shard_map/isl,stlj->itj/dot_general | solution.py:19
  531.3 0.0 reduce-scatter.8.cloned.1.call-update
  531.3 72.5 %reduce-scatter.8.cloned.1.call-done = f32[16,12,128]{2,0,1:T(8,128)} async-done(((f32[128,12,128]{2,0,1:T(8,128)}), f32[16,12,128]{2,0,1:T(8,128)}) %reduce-scatter.8.cloned.1.call-update) | async-done | bytes 98320 | tf_op jit(solution)/shard_map/reduce_scatter | solution.py:47
  603.8 1.1 fusion.20
  604.9 0.7 pad_maximum_fusion
Async XLA Ops:
  6.5 201.3 %copy-start = (f32[128,128]{1,0:T(8,128)S(1)}, f32[128,128]{1,0:T(8,128)}, u32[]{:S(2)}) copy-start(f32[128,128]{1,0:T(8,128)} %param.5) | copy-start | bytes 196612
  6.5 201.3 %copy-start.1 = (f32[16,12,128]{2,0,1:T(8,128)S(1)}, f32[16,12,128]{2,0,1:T(8,128)}, u32[]{:S(2)}) copy-start(f32[16,12,128]{2,0,1:T(8,128)} %param.3) | copy-start | bytes 294916
  6.5 114.4 %all-gather.4.cloned.1.call-start = ((), (), s32[]{:S(2)}) async-start(), calls=%async_computation.3 | async-start | bytes 13369344 | tf_op jit(solution)/shard_map/all_gather | solution.py:14
  46.2 161.7 %reduce-scatter.4.cloned.1.call-start = ((), (), s32[]{:S(2)}) async-start(), calls=%async_computation.4 | async-start | bytes 884736 | tf_op jit(solution)/shard_map/reduce_scatter | solution.py:47
  135.3 183.6 %all-gather.6.cloned.1.call-start = ((), (), s32[]{:S(2)}) async-start(), calls=%async_computation.5 | async-start | bytes 13369344 | tf_op jit(solution)/shard_map/all_gather | solution.py:14
  247.9 157.9 %reduce-scatter.6.cloned.1.call-start = ((), (), s32[]{:S(2)}) async-start(), calls=%async_computation.6 | async-start | bytes 884736 | tf_op jit(solution)/shard_map/reduce_scatter | solution.py:47
  333.3 183.6 %all-gather.8.cloned.1.call-start = ((), (), s32[]{:S(2)}) async-start(), calls=%async_computation.7 | async-start | bytes 13369344 | tf_op jit(solution)/shard_map/all_gather | solution.py:14
  445.9 157.9 %reduce-scatter.8.cloned.1.call-start = ((), (), s32[]{:S(2)}) async-start(), calls=%async_computation.8 | async-start | bytes 884736 | tf_op jit(solution)/shard_map/reduce_scatter | solution.py:47
Sparse Core Ops, SparseCore 0:
  46.3 74.6 all-gather.3
  135.4 72.3 reduce-scatter.3
  248.1 70.8 all-gather.5
  333.4 72.3 reduce-scatter.5
  446.1 70.8 all-gather.7
  531.4 72.3 reduce-scatter.7
where the time goes:
time: 613 us
  waiting for transfers between devices  434 us (71%)
  blocking collectives  116 us (19%)
  matrix products  46.4 us (8%)
  between operations  13.5 us (2%)
    reduce_scatter x3, waiting for transfers between devices, per_device(): lax.psum_scatter(contract(sigma_rows, history), 'row', scatter_dimension=...  217 us
    all_gather x3, waiting for transfers between devices, sigma_panel(): gathered = lax.all_gather(sigma_all, 'col', axis=1, tiled=True)  216 us
    all_gather x3, blocking collectives, per_device(): sigma_all = lax.all_gather(sigma_local, 'row', axis=0, tiled=True)  116 us
    dot_general x3, matrix products, contract(): jnp.einsum('isl,stlj->itj', sigma_rows, history, precision=lax.Precision....  43 us
  transfers between devices with their start and end apart: 6, of which 6 were waited for; matrix products, arithmetic and copies ran while one was open for 0% of the time, Pallas kernels for 0%

commit v1 on v0

v1 whole, which is shorter than its diff:
```python
import jax
import jax.numpy as jnp
from jax import lax
from jax.experimental import pallas as pl
from jax.experimental.pallas import tpu as pltpu
from jax.sharding import PartitionSpec as P

STEPS = 3
time_step = 0.2
MESH = pl.DeviceIdType.MESH
bf16, f32 = jnp.bfloat16, jnp.float32
GROUP = 8
HALVES = 2
SUB = 8
TIMES = 12
ORB = 128
LANES = TIMES * ORB
DEPTH = 2 * LANES
PAIRS = TIMES // 2
SLOTS = 8
TILES = 24


def kernel(
    x_ref, ham_ref, hist_ref, out_ref,
    staged, hist_hi, hist_lo, operand, partial, arrived, sigma, mine, current,
    load_sem, sums_send, sums_recv, turn_send, turn_recv, wide_send, wide_recv, pair_send, pair_recv,
):
    row = lax.axis_index("row")
    col = lax.axis_index("col")
    chip = col // 2
    core = col % 2
    diagonal = row == chip
    off_diagonal = jnp.logical_not(diagonal)

    def load(tile):
        slot = lax.rem(tile, SLOTS)
        return pltpu.make_async_copy(hist_ref.at[tile], staged.at[slot], load_sem.at[slot])

    for tile in range(SLOTS):
        load(tile).start()

    def at(r, c, k):
        return (r, c * 2 + k)

    barrier = pltpu.get_barrier_semaphore()

    def greet(device):
        pl.semaphore_signal(barrier, inc=1, device_id=device, device_id_type=MESH)

    for m in range(1, GROUP):
        greet(at(lax.rem(row + m, GROUP), chip, core))
        greet(at(row, lax.rem(chip + m, GROUP), core))
    greet(at(row, chip, 1 - core))

    @pl.when(off_diagonal)
    def _():
        greet(at(chip, row, core))

    pl.semaphore_wait(barrier, 2 * (GROUP - 1) + 1 + jnp.where(diagonal, 0, 1))

    def rows_of(block):
        return pl.ds(pl.multiple_of(block * SUB, SUB), SUB)

    def turn(k, h):
        return pltpu.make_async_remote_copy(
            src_ref=mine.at[k, h],
            dst_ref=sigma.at[k, h, core, rows_of(row)],
            send_sem=turn_send.at[k, h],
            recv_sem=turn_recv.at[k, h],
            device_id=at(chip, row, core),
            device_id_type=MESH,
        )

    def start_turn(k, h):
        value = current[h]
        cubed = value * value * value

        @pl.when(off_diagonal)
        def _():
            mine[k, h] = cubed
            turn(k, h).start()

        @pl.when(diagonal)
        def _():
            sigma[k, h, core, rows_of(row)] = cubed

    def widen(k, h):
        @pl.when(off_diagonal)
        def _():
            turn(k, h).wait_recv()

        part = sigma.at[k, h, core, rows_of(chip)]
        for m in range(1, GROUP):
            pltpu.make_async_remote_copy(
                src_ref=part,
                dst_ref=part,
                send_sem=wide_send.at[k, h],
                recv_sem=wide_recv.at[k, h],
                device_id=at(row, lax.rem(chip + m, GROUP), core),
                device_id_type=MESH,
            ).start()

    def seven(k, h):
        return sigma.at[k, h, core, pl.ds(0, (GROUP - 1) * SUB)]

    def share(k, h):
        return pltpu.make_async_remote_copy(
            src_ref=sigma.at[k, h, core],
            dst_ref=sigma.at[k, h, core],
            send_sem=pair_send.at[k, h],
            recv_sem=pair_recv.at[k, h],
            device_id=at(row, chip, 1 - core),
            device_id_type=MESH,
        )

    def start_share(k, h):
        pltpu.make_async_copy(seven(k, h), seven(k, h), wide_recv.at[k, h]).wait()
        share(k, h).start()

    def split(tile, _):
        load(tile).wait()
        slot = lax.rem(tile, SLOTS)
        depth = pl.ds(pl.multiple_of(tile * ORB, ORB), ORB)

        def one(pair, _):
            for q in range(2):
                value = staged[slot, pair * 2 + q]
                hi = value.astype(bf16)
                lo = (value - hi.astype(f32)).astype(bf16)
                hist_hi[pair, depth, q * ORB:(q + 1) * ORB] = hi
                hist_lo[pair, depth, q * ORB:(q + 1) * ORB] = lo
            return 0

        lax.fori_loop(0, PAIRS, one, 0)

        @pl.when(tile + SLOTS < TILES)
        def _():
            load(tile + SLOTS).start()

        return 0

    def send_sums(k, h, lanes):
        for m in range(1, GROUP):
            other = lax.rem(row + m, GROUP)
            pltpu.make_async_remote_copy(
                src_ref=partial.at[k, h, rows_of(other), lanes],
                dst_ref=arrived.at[k, h, row, :, lanes],
                send_sem=sums_send.at[k, h],
                recv_sem=sums_recv.at[k, h],
                device_id=at(other, chip, core),
                device_id_type=MESH,
            ).start()

    def contract(k, h):
        share(k, h).wait_recv()
        for c in range(2):
            value = sigma[k, h, c]
            hi = value.astype(bf16)
            operand[0:64, c * LANES:(c + 1) * LANES] = hi
            operand[64:128, c * LANES:(c + 1) * LANES] = (value - hi.astype(f32)).astype(bf16)

        def one(pair, _):
            both = jnp.dot(operand[...], hist_hi[pair], preferred_element_type=f32)
            low = jnp.dot(operand[0:64], hist_lo[pair], preferred_element_type=f32)
            lanes = pl.ds(pl.multiple_of(pair * 256, 256), 256)
            partial[k, h, :, lanes] = both[0:64] + (both[64:128] + low)
            return 0

        lax.fori_loop(0, PAIRS // 2, one, 0)
        send_sums(k, h, pl.ds(0, LANES // 2))
        lax.fori_loop(PAIRS // 2, PAIRS, one, 0)
        send_sums(k, h, pl.ds(LANES // 2, LANES // 2))

    def advance(k, h):
        value = current[h]
        stacked = jnp.concatenate([value[:, t * ORB:(t + 1) * ORB] for t in range(TIMES)], axis=0)
        kinetic = jnp.dot(stacked, ham_ref[...], precision=lax.Precision.HIGHEST, preferred_element_type=f32)
        kinetic = jnp.concatenate([kinetic[t * SUB:(t + 1) * SUB] for t in range(TIMES)], axis=1)
        got = arrived.at[k, h, pl.ds(0, GROUP - 1)]
        pltpu.make_async_copy(got, got, sums_recv.at[k, h]).wait()
        total = partial[k, h, rows_of(row)]
        for m in range(1, GROUP):
            total += arrived[k, h, lax.rem(row + m, GROUP)]
        value = value - time_step * (kinetic + total)
        current[h] = value
        for t in range(TIMES):
            out_ref[k, t, h * SUB:(h + 1) * SUB] = value[:, t * ORB:(t + 1) * ORB]

    for h in range(HALVES):
        for t in range(TIMES):
            current[h, :, t * ORB:(t + 1) * ORB] = x_ref[t, h * SUB:(h + 1) * SUB]
        start_turn(0, h)
    lax.fori_loop(0, 8, split, 0)
    for h in range(HALVES):
        widen(0, h)
    lax.fori_loop(8, TILES, split, 0)
    start_share(0, 0)

    def step(k, _):
        start_share(k, 1)
        contract(k, 0)
        contract(k, 1)
        advance(k, 0)

        @pl.when(k < STEPS - 1)
        def _():
            start_turn(k + 1, 0)
            widen(k + 1, 0)

        advance(k, 1)

        @pl.when(k < STEPS - 1)
        def _():
            start_turn(k + 1, 1)
            widen(k + 1, 1)
            start_share(k + 1, 0)

        return 0

    lax.fori_loop(0, STEPS, step, 0)

    def drain(k, _):
        for h in range(HALVES):
            sent = partial.at[k, h, pl.ds(0, (GROUP - 1) * SUB)]
            pltpu.make_async_copy(sent, sent, sums_send.at[k, h]).wait()
            pltpu.make_async_copy(seven(k, h), seven(k, h), wide_send.at[k, h]).wait()
            share(k, h).wait_send()

            @pl.when(off_diagonal)
            def _():
                turn(k, h).wait_send()

        return 0

    lax.fori_loop(0, STEPS, drain, 0)


def per_device(new_row, history, hamiltonian):
    owned = jnp.transpose(new_row, (1, 0, 2))
    dma = pltpu.SemaphoreType.DMA
    out = pl.pallas_call(
        kernel,
        out_shape=jax.ShapeDtypeStruct((STEPS, TIMES, HALVES * SUB, ORB), f32),
        in_specs=[
            pl.BlockSpec(memory_space=pltpu.VMEM),
            pl.BlockSpec(memory_space=pltpu.VMEM),
            pl.BlockSpec(memory_space=pl.ANY),
        ],
        out_specs=pl.BlockSpec(memory_space=pltpu.VMEM),
        scratch_shapes=[
            pltpu.VMEM((SLOTS, TIMES, ORB, ORB), f32),
            pltpu.VMEM((PAIRS, DEPTH, 256), bf16),
            pltpu.VMEM((PAIRS, DEPTH, 256), bf16),
            pltpu.VMEM((128, DEPTH), bf16),
            pltpu.VMEM((STEPS, HALVES, GROUP * SUB, LANES), f32),
            pltpu.VMEM((STEPS, HALVES, GROUP, SUB, LANES), f32),
            pltpu.VMEM((STEPS, HALVES, 2, GROUP * SUB, LANES), f32),
            pltpu.VMEM((STEPS, HALVES, SUB, LANES), f32),
            pltpu.VMEM((HALVES, SUB, LANES), f32),
            dma((SLOTS,)),
        ] + [dma((STEPS, HALVES))] * 8,
        compiler_params=pltpu.CompilerParams(
            collective_id=0, has_side_effects=True, vmem_limit_bytes=56 << 20
        ),
        cost_estimate=pl.CostEstimate(flops=11_000_000_000, bytes_accessed=20_000_000, transcendentals=0),
    )(owned, hamiltonian, history)
    return jnp.transpose(out, (0, 2, 1, 3))


def solution(mesh):
    placed = (P("row", "col", None), P("row", "col", None, None), P())
    return jax.shard_map(
        per_device,
        mesh=mesh,
        in_specs=placed,
        out_specs=P(None, "row", "col", None),
        check_vma=False,
    )
```

time: 613 us -> 95.8 us (0.16)
  waiting for transfers between devices: 434 us -> 0 us
  blocking collectives: 116 us -> 0 us
  Pallas kernels: 0 us -> 93.9 us
  matrix products: 46.4 us -> 0 us
  between operations: 13.5 us -> 0.01 us
    reduce_scatter x3 -> x0, waiting for transfers between devices: 217 us -> none  [per_device(): lax.psum_scatter(contract(sigma_rows, history), 'row', scatter_dimension=...]
    all_gather x3 -> x0, waiting for transfers between devices: 216 us -> none  [sigma_panel(): gathered = lax.all_gather(sigma_all, 'col', axis=1, tiled=True)]
    all_gather x3 -> x0, blocking collectives: 116 us -> none  [per_device(): sigma_all = lax.all_gather(sigma_local, 'row', axis=0, tiled=True)]
    pallas_call x0 -> x1, Pallas kernels: none -> 93.9 us  [per_device(): pl.pallas_call(kernel, out_shape=jax.ShapeDtypeStruct((STEPS, TIMES, HALV...]
    dot_general x6 -> x0, matrix products: 46.4 us -> none  [the longest x3 43 us: contract(): jnp.einsum('isl,stlj->itj', sigma_rows, history, precision=lax.Precision....]
  transfers between devices with their start and end apart: 6 -> 0, of which waited for: 6 -> 0; matrix products, arithmetic and copies ran while one was open for 0% -> 0% of each run, Pallas kernels for 0% -> 0%
where the time goes in v1:
time: 95.8 us; the launch traced here: 95.6 us
  Pallas kernels  93.9 us (98%)
  local copies, waits for them, and re-layouts  1.69 us (2%)
    pallas_call x1, Pallas kernels, per_device(): pl.pallas_call(kernel, out_shape=jax.ShapeDtypeStruct((STEPS, TIMES, HALV...  93.9 us

profile of v1, /device:TPU:0, one launch (start us, length us, event | category | flops | bytes accessed | tf_op | source)
XLA Modules:
  0.0 95.6 jit_solution(9967569861145190195)
XLA Ops:
  0.0 93.9 %shard_map.37 = f32[3,12,16,128]{3,2,1,0:T(8,128)} custom-call(f32[12,16,128]{2,1,0:T(8,128)} %bitcast.3, f32[128,128]{1,0:T(8,128)} %ham_ref.1, f32[24,12,128,128]{3,2,1,0:T(8,128)} %hist_ref.1), custom_call_target="tpu_custom_call" | custom-call | flops 11000000512 | bytes 20000000 | tf_op jit(solution)/shard_map/pallas_call | solution.py:242
  93.9 1.7 %copy.5 = f32[3,16,12,128]{3,1,2,0:T(8,128)} copy(f32[3,16,12,128]{3,1,2,0:T(8,128)} %bitcast.2) | data formatting | bytes 589824

commit v2 on v1

v2 whole, which is shorter than its diff:
```python
import jax
import jax.numpy as jnp
from jax import lax
from jax.experimental import pallas as pl
from jax.experimental.pallas import tpu as pltpu
from jax.sharding import PartitionSpec as P

STEPS = 3
time_step = 0.2
MESH = pl.DeviceIdType.MESH
bf16, f32 = jnp.bfloat16, jnp.float32
GROUP = 8
CHAINS = 2
CHUNKS = 2
SUB = 16 // CHAINS
ROWS = GROUP * SUB
TIMES = 12
ORB = 128
WIDE = TIMES * ORB // CHUNKS
DEPTH = 2 * TIMES * ORB
PER = TIMES // CHUNKS
PAIRS = TIMES // 2
SLOTS = 8
TILES = 24
UNROLL = 3
AFTER = 0
LATE = 14
EARLY = 8


def kernel(
    x_ref, ham_ref, hist_ref, out_ref,
    staged, hist_hi, hist_lo, operand, partial, arrived, sigma, mine, current,
    load_sem, sums_send, sums_recv, turn_send, turn_recv, wide_send, wide_recv, pair_send, pair_recv,
):
    row = lax.axis_index("row")
    col = lax.axis_index("col")
    chip = col // 2
    core = col % 2
    diagonal = row == chip
    off_diagonal = jnp.logical_not(diagonal)
    pieces = [(h, g) for h in range(CHAINS) for g in range(CHUNKS)]

    def load(tile):
        slot = lax.rem(tile, SLOTS)
        return pltpu.make_async_copy(hist_ref.at[tile], staged.at[slot], load_sem.at[slot])

    for tile in range(SLOTS):
        load(tile).start()

    def at(r, c, k):
        return (r, c * 2 + k)

    def remote(src, dst, send, recv, device):
        return pltpu.make_async_remote_copy(
            src_ref=src, dst_ref=dst, send_sem=send, recv_sem=recv, device_id=device, device_id_type=MESH
        )

    def wait_bytes(ref, sem):
        pltpu.make_async_copy(ref, ref, sem).wait()

    barrier = pltpu.get_barrier_semaphore()

    def greet(device):
        pl.semaphore_signal(barrier, inc=1, device_id=device, device_id_type=MESH)

    for m in range(1, GROUP):
        greet(at(lax.rem(row + m, GROUP), chip, core))
        greet(at(row, lax.rem(chip + m, GROUP), core))
    greet(at(row, chip, 1 - core))

    @pl.when(off_diagonal)
    def _():
        greet(at(chip, row, core))

    def rows_of(block, count=SUB):
        return pl.ds(pl.multiple_of(block * count, count), count)

    pl.semaphore_wait(barrier, 2 * (GROUP - 1) + 1 + jnp.where(diagonal, 0, 1))

    def turn(k, h, g):
        return remote(
            mine.at[k, h, g], sigma.at[k, h, g, core, rows_of(row)], turn_send.at[k, h, g], turn_recv.at[k, h, g],
            at(chip, row, core),
        )

    def start_turn(k, h, g):
        value = current[h, g]
        cubed = value * value * value

        @pl.when(off_diagonal)
        def _():
            mine[k, h, g] = cubed
            turn(k, h, g).start()

        @pl.when(diagonal)
        def _():
            sigma[k, h, g, core, rows_of(row)] = cubed

    def widen(k, h, g):
        pl.when(off_diagonal)(turn(k, h, g).wait_recv)
        part = sigma.at[k, h, g, core, rows_of(chip)]
        for m in range(1, GROUP):
            remote(
                part, part, wide_send.at[k, h, g], wide_recv.at[k, h, g], at(row, lax.rem(chip + m, GROUP), core)
            ).start()

    def most(k, h, g):
        return sigma.at[k, h, g, core, pl.ds(0, (GROUP - 1) * SUB)]

    def share(k, h, g):
        whole = sigma.at[k, h, g, core]
        return remote(whole, whole, pair_send.at[k, h, g], pair_recv.at[k, h, g], at(row, chip, 1 - core))

    def start_share(k, h, g):
        wait_bytes(most(k, h, g), wide_recv.at[k, h, g])
        share(k, h, g).start()

    def split(tile, _):
        load(tile).wait()
        slot = lax.rem(tile, SLOTS)
        half, time = tile // TIMES, tile % TIMES
        offset = (time // PER) * (2 * WIDE) + half * WIDE + (time % PER) * ORB
        depth = pl.ds(pl.multiple_of(offset, ORB), ORB)

        def one(pair, _):
            for q in range(2):
                value = staged[slot, pair * 2 + q]
                hi = value.astype(bf16)
                lo = (value - hi.astype(f32)).astype(bf16)
                hist_hi[pair, depth, q * ORB:(q + 1) * ORB] = hi
                hist_lo[pair, depth, q * ORB:(q + 1) * ORB] = lo
            return 0

        lax.fori_loop(0, PAIRS, one, 0)

        @pl.when(tile + SLOTS < TILES)
        def _():
            load(tile + SLOTS).start()

        return 0

    def send_sums(k, h, g):
        for m in range(1, GROUP):
            other = lax.rem(row + m, GROUP)
            remote(
                partial.at[k, h, g, rows_of(other)], arrived.at[k, h, g, row], sums_send.at[k, h, g],
                sums_recv.at[k, h, g], at(other, chip, core),
            ).start()

    def contract(k, h, between):
        for g in range(CHUNKS):
            share(k, h, g).wait_recv()
            for c in range(2):
                value = sigma[k, h, g, c]
                hi = value.astype(bf16)
                lanes = slice((2 * g + c) * WIDE, (2 * g + c + 1) * WIDE)
                operand[0:ROWS, lanes] = hi
                operand[ROWS:2 * ROWS, lanes] = (value - hi.astype(f32)).astype(bf16)
            depth = slice(2 * g * WIDE, 2 * (g + 1) * WIDE)

            def part(target):
                def one(p, _):
                    pair = target * (PER // 2) + p
                    both = jnp.dot(operand[:, depth], hist_hi[pair, depth], preferred_element_type=f32)
                    low = jnp.dot(operand[0:ROWS, depth], hist_lo[pair, depth], preferred_element_type=f32)
                    lanes = pl.ds(pl.multiple_of(p * 256, 256), 256)
                    total = both[0:ROWS] + (both[ROWS:2 * ROWS] + low)
                    if g > 0:
                        total += partial[k, h, target, :, lanes]
                    partial[k, h, target, :, lanes] = total
                    return 0

                lax.fori_loop(0, PER // 2, one, 0, unroll=UNROLL)

            if g < CHUNKS - 1:
                def every(target, _):
                    part(target)
                    return 0

                lax.fori_loop(0, CHUNKS, every, 0)
            else:
                for target in range(CHUNKS):
                    part(target)
                    send_sums(k, h, target)
                    between(target)

    def kinetic(value):
        stacked = jnp.concatenate([value[:, t * ORB:(t + 1) * ORB] for t in range(PER)], axis=0)
        moved = jnp.dot(stacked, ham_ref[...], precision=lax.Precision.HIGHEST, preferred_element_type=f32)
        return jnp.concatenate([moved[t * SUB:(t + 1) * SUB] for t in range(PER)], axis=1)

    def advance(k, h, g):
        value = current[h, g]
        moved = kinetic(value)
        wait_bytes(arrived.at[k, h, g, pl.ds(0, GROUP - 1)], sums_recv.at[k, h, g])
        total = partial[k, h, g, rows_of(row)]
        for m in range(1, GROUP):
            total += arrived[k, h, g, lax.rem(row + m, GROUP)]
        value = value - time_step * (moved + total)
        current[h, g] = value
        for t in range(PER):
            out_ref[k, g * PER + t, h * SUB:(h + 1) * SUB] = value[:, t * ORB:(t + 1) * ORB]

    for h, g in pieces:
        for t in range(PER):
            current[h, g, :, t * ORB:(t + 1) * ORB] = x_ref[g * PER + t, h * SUB:(h + 1) * SUB]
        start_turn(0, h, g)
    lax.fori_loop(0, EARLY, split, 0)
    for g in range(CHUNKS):
        widen(0, 0, g)
    lax.fori_loop(EARLY, LATE, split, 0)
    for g in range(CHUNKS):
        widen(0, 1, g)
    lax.fori_loop(LATE, TILES, split, 0)
    for g in range(CHUNKS):
        start_share(0, 0, g)

    def step(k, _):
        def between(target):
            if target == AFTER:
                for g in range(CHUNKS):
                    start_share(k, 1, g)

        contract(k, 0, between)
        contract(k, 1, lambda target: None)

        @pl.when(k < STEPS - 1)
        def _():
            for h in range(CHAINS):
                for g in range(CHUNKS):
                    advance(k, h, g)
                    start_turn(k + 1, h, g)
            for h in range(CHAINS):
                for g in range(CHUNKS):
                    widen(k + 1, h, g)
            for g in range(CHUNKS):
                start_share(k + 1, 0, g)

        @pl.when(k == STEPS - 1)
        def _():
            for h, g in pieces:
                advance(k, h, g)

        return 0

    lax.fori_loop(0, STEPS, step, 0)

    def drain(k, _):
        for h, g in pieces:
            wait_bytes(partial.at[k, h, g, pl.ds(0, (GROUP - 1) * SUB)], sums_send.at[k, h, g])
            wait_bytes(most(k, h, g), wide_send.at[k, h, g])
            share(k, h, g).wait_send()
            pl.when(off_diagonal)(turn(k, h, g).wait_send)
        return 0

    lax.fori_loop(0, STEPS, drain, 0)

def per_device(new_row, history, hamiltonian):
    dma = pltpu.SemaphoreType.DMA
    each = (CHAINS, CHUNKS)
    steps = (STEPS,) + each
    out = pl.pallas_call(
        kernel,
        out_shape=jax.ShapeDtypeStruct((STEPS, TIMES, 16, ORB), f32),
        in_specs=[
            pl.BlockSpec(memory_space=pltpu.VMEM),
            pl.BlockSpec(memory_space=pltpu.VMEM),
            pl.BlockSpec(memory_space=pl.ANY),
        ],
        out_specs=pl.BlockSpec(memory_space=pltpu.VMEM),
        scratch_shapes=[
            pltpu.VMEM((SLOTS, TIMES, ORB, ORB), f32),
            pltpu.VMEM((PAIRS, DEPTH, 256), bf16),
            pltpu.VMEM((PAIRS, DEPTH, 256), bf16),
            pltpu.VMEM((2 * ROWS, DEPTH), bf16),
            pltpu.VMEM(steps + (ROWS, WIDE), f32),
            pltpu.VMEM(steps + (GROUP, SUB, WIDE), f32),
            pltpu.VMEM(steps + (2, ROWS, WIDE), f32),
            pltpu.VMEM(steps + (SUB, WIDE), f32),
            pltpu.VMEM(each + (SUB, WIDE), f32),
            dma((SLOTS,)),
        ] + [dma(steps)] * 8,
        compiler_params=pltpu.CompilerParams(
            collective_id=0, has_side_effects=True, vmem_limit_bytes=58 << 20
        ),
        cost_estimate=pl.CostEstimate(flops=11_000_000_000, bytes_accessed=20_000_000, transcendentals=0),
    )(jnp.transpose(new_row, (1, 0, 2)), hamiltonian, history)
    return jnp.transpose(out, (0, 2, 1, 3))


def solution(mesh):
    placed = (P("row", "col", None), P("row", "col", None, None), P())
    return jax.shard_map(
        per_device,
        mesh=mesh,
        in_specs=placed,
        out_specs=P(None, "row", "col", None),
        check_vma=False,
    )
```

time: 95.8 us -> 91.2 us (0.952)
  Pallas kernels: 93.9 us -> 88.9 us
    pallas_call x1, Pallas kernels: 93.9 us -> 88.9 us  [per_device(): pl.pallas_call(kernel, out_shape=jax.ShapeDtypeStruct((STEPS, TIMES, 16,...]
where the time goes in v2:
time: 91.2 us; the launch traced here: 90.6 us
  Pallas kernels  88.9 us (97%)
  local copies, waits for them, and re-layouts  1.69 us (2%)
    pallas_call x1, Pallas kernels, per_device(): pl.pallas_call(kernel, out_shape=jax.ShapeDtypeStruct((STEPS, TIMES, 16,...  88.9 us

profile of v2, /device:TPU:0, one launch (start us, length us, event | category | flops | bytes accessed | tf_op | source)
XLA Modules:
  0.0 90.6 jit_solution(7162793817655576576)
XLA Ops:
  0.0 88.9 %shard_map.37 = f32[3,12,16,128]{3,2,1,0:T(8,128)} custom-call(f32[12,16,128]{2,1,0:T(8,128)} %bitcast.3, f32[128,128]{1,0:T(8,128)} %ham_ref.1, f32[24,12,128,128]{3,2,1,0:T(8,128)} %hist_ref.1), custom_call_target="tpu_custom_call" | custom-call | flops 11000000512 | bytes 20000000 | tf_op jit(solution)/shard_map/pallas_call | solution.py:263
  88.9 1.7 %copy.5 = f32[3,16,12,128]{3,1,2,0:T(8,128)} copy(f32[3,16,12,128]{3,1,2,0:T(8,128)} %bitcast.2) | data formatting | bytes 589824

commit v3 on v2

--- a/solution.py
+++ b/solution.py
@@ -23,7 +23,6 @@
 SLOTS = 8
 TILES = 24
 UNROLL = 3
-AFTER = 0
 LATE = 14
 EARLY = 8
 
@@ -76,6 +75,10 @@
     def rows_of(block, count=SUB):
         return pl.ds(pl.multiple_of(block * count, count), count)
 
+    for h, g in pieces:
+        for t in range(PER):
+            current[h, g, :, t * ORB:(t + 1) * ORB] = x_ref[g * PER + t, h * SUB:(h + 1) * SUB]
+
     pl.semaphore_wait(barrier, 2 * (GROUP - 1) + 1 + jnp.where(diagonal, 0, 1))
 
     def turn(k, h, g):
@@ -203,8 +206,6 @@
             out_ref[k, g * PER + t, h * SUB:(h + 1) * SUB] = value[:, t * ORB:(t + 1) * ORB]
 
     for h, g in pieces:
-        for t in range(PER):
-            current[h, g, :, t * ORB:(t + 1) * ORB] = x_ref[g * PER + t, h * SUB:(h + 1) * SUB]
         start_turn(0, h, g)
     lax.fori_loop(0, EARLY, split, 0)
     for g in range(CHUNKS):
@@ -218,9 +219,7 @@
 
     def step(k, _):
         def between(target):
-            if target == AFTER:
-                for g in range(CHUNKS):
-                    start_share(k, 1, g)
+            start_share(k, 1, target)
 
         contract(k, 0, between)
         contract(k, 1, lambda target: None)

time: 91.2 us -> 91.3 us (level)
  no operation moved by 1% of the time
where the time goes in v3:
time: 91.3 us; the launch traced here: 90.8 us
  Pallas kernels  89.1 us (98%)
  local copies, waits for them, and re-layouts  1.69 us (2%)
    pallas_call x1, Pallas kernels, per_device(): pl.pallas_call(kernel, out_shape=jax.ShapeDtypeStruct((STEPS, TIMES, 16,...  89.1 us

profile of v3, /device:TPU:0, one launch (start us, length us, event | category | flops | bytes accessed | tf_op | source)
XLA Modules:
  0.0 90.8 jit_solution(868631212021242964)
XLA Ops:
  0.0 89.1 %shard_map.37 = f32[3,12,16,128]{3,2,1,0:T(8,128)} custom-call(f32[12,16,128]{2,1,0:T(8,128)} %bitcast.3, f32[128,128]{1,0:T(8,128)} %ham_ref.1, f32[24,12,128,128]{3,2,1,0:T(8,128)} %hist_ref.1), custom_call_target="tpu_custom_call" | custom-call | flops 11000000512 | bytes 20000000 | tf_op jit(solution)/shard_map/pallas_call | solution.py:262
  89.1 1.7 %copy.5 = f32[3,16,12,128]{3,1,2,0:T(8,128)} copy(f32[3,16,12,128]{3,1,2,0:T(8,128)} %bitcast.2) | data formatting | bytes 589824
